TPU v7x, 128 devices: a whole 4x4x4 slice. The times are simulated.
128 devices in a mesh: gx: 8 (over x, core), gy: 16 (over y, z).
Axes of the slice: x: 4, y: 4, z: 4, core: 2. Of those that a mesh axis runs over, the one named last changes fastest.
Arguments:
- coverage: int32 [8192, 8192], P('gx', 'gy'), may hold values from 0 to 64, as said below
- dose: float32 [8192, 8192], P('gx', 'gy'), may hold values from 0.5 to 2, as said below
Outputs:
- dose_map: float32 [8192, 8192], P('gx', 'gy')
- residual: float32 [8192, 8192], P('gx', 'gy')
Inputs may be any that keep to these rules, and one draw needn't show every extreme that they name: coverage counts 64ths of a cell's area. `dose`: doses are positive.
All inputs are finite; a program needn't handle non-finite values.
Results may differ from a plain program's by a relative error of at most 0.0001.
Values sent between devices are 32-bit elements; how exact they have to be, the bound alone decides.
A program may use at most 64 MiB of HBM per device.

v0:
```python
import math

import jax
import jax.numpy as jnp
from jax import lax
from jax.sharding import PartitionSpec as P

RIM = 30
COARSE = 1024
FOG = 3072
ITERS = 6


def padded_2(block, sides, width):
    for axis, dim in sides:
        count = lax.axis_size(axis)
        forward = [(i, i + 1) for i in range(count - 1)]
        backward = [(target, source) for source, target in forward]
        low = lax.ppermute(
            lax.slice_in_dim(block, block.shape[dim] - width, None, axis=dim), axis, forward
        )
        high = lax.ppermute(lax.slice_in_dim(block, 0, width, axis=dim), axis, backward)
        block = jnp.concatenate([low, block, high], axis=dim)
    return block


def choose_block():
    return 256


def band_matrix(block_size):
    row_index = jnp.arange(block_size + 2 * RIM)[:, None]
    col_index = jnp.arange(block_size)[None, :]
    offset = (row_index - col_index - RIM).astype(jnp.float32)
    tap_offsets = jnp.arange(-RIM, RIM + 1).astype(jnp.float32)
    tap_total = jnp.sum(jnp.exp(-tap_offsets * tap_offsets / 200.0))
    weights = jnp.exp(-offset * offset / 200.0) / tap_total
    return jnp.where(jnp.abs(offset) <= RIM, weights, 0.0)


def fog_rows_of(first_index, local_count, total_count):
    sigma = FOG / COARSE
    local_pos = (first_index + jnp.arange(local_count)).astype(jnp.float32)[:, None]
    every_pos = jnp.arange(total_count).astype(jnp.float32)[None, :]
    spread = local_pos - every_pos
    return jnp.exp(-spread * spread / (2.0 * sigma * sigma)) / (math.sqrt(2.0 * math.pi) * sigma)


def blur_second(padded, band, block_size, block_count):
    pieces = []
    for number in range(block_count):
        window = padded[:, number * block_size : number * block_size + block_size + 2 * RIM]
        pieces.append(jnp.dot(window, band, precision=lax.Precision.HIGHEST))
    return jnp.concatenate(pieces, axis=1)


def blur_first(padded, band, block_size, block_count):
    pieces = []
    for number in range(block_count):
        window = padded[number * block_size : number * block_size + block_size + 2 * RIM, :]
        pieces.append(jnp.dot(band.T, window, precision=lax.Precision.HIGHEST))
    return jnp.concatenate(pieces, axis=0)


def per_device(coverage, dose):
    fraction = coverage.astype(jnp.float32) / 64.0
    height, breadth = dose.shape
    first_block = choose_block()
    second_block = choose_block()
    band_first = band_matrix(first_block)
    band_second = band_matrix(second_block)
    rows_local = max(1, height // COARSE)
    rows_span = min(height, COARSE)
    cols_local = max(1, breadth // COARSE)
    cols_span = min(breadth, COARSE)
    group_first = max(1, COARSE // height)
    group_second = max(1, COARSE // breadth)
    total_first = height * lax.axis_size("gx") // COARSE
    total_second = breadth * lax.axis_size("gy") // COARSE
    fog_first = fog_rows_of(lax.axis_index("gx") * height // COARSE, rows_local, total_first)
    fog_second = fog_rows_of(lax.axis_index("gy") * breadth // COARSE, cols_local, total_second)
    dose_map = dose
    residual = jnp.zeros_like(dose)
    for step in range(ITERS):
        charge = fraction * dose_map
        padded = padded_2(charge, (("gx", 0), ("gy", 1)), RIM)
        partial_blur = blur_second(padded, band_second, second_block, breadth // second_block)
        back = blur_first(partial_blur, band_first, first_block, height // first_block)
        block_share = charge.reshape(rows_local, rows_span, cols_local, cols_span).sum(
            axis=(1, 3)
        ) / float(COARSE * COARSE)
        gathered = lax.all_gather(block_share, ("gx", "gy"), axis=0, tiled=True)
        grid_parts = gathered.reshape(
            lax.axis_size("gx"), lax.axis_size("gy"), rows_local, cols_local
        )
        grid_parts = grid_parts.transpose(0, 2, 1, 3).reshape(
            lax.axis_size("gx") * rows_local, lax.axis_size("gy") * cols_local
        )
        coarse_grid = grid_parts.reshape(total_first, group_first, total_second, group_second).sum(
            axis=(1, 3)
        )
        fog = jnp.dot(
            jnp.dot(fog_first, coarse_grid, precision=lax.Precision.HIGHEST),
            fog_second.T,
            precision=lax.Precision.HIGHEST,
        )
        fog_fine = jnp.broadcast_to(
            fog[:, None, :, None], (rows_local, rows_span, cols_local, cols_span)
        ).reshape(height, breadth)
        energy = (charge + 0.7 * back + 0.3 * fog_fine) / 2.0
        residual = 0.5 - energy
        dose_map = dose_map + 1.5 * residual
    return (dose_map, residual)


def solution(mesh):
    return jax.shard_map(
        per_device,
        mesh=mesh,
        in_specs=(P("gx", "gy"), P("gx", "gy")),
        out_specs=(P("gx", "gy"), P("gx", "gy")),
        check_vma=False,
    )
```

profile of v0, /device:TPU:1, one launch (start us, length us, event | category | flops | bytes accessed | tf_op | source)
XLA Modules:
  0.0 689.3 jit_solution(12506968471591964709)
XLA Ops:
  0.6 3.4 fusion.394
  4.1 4.5 collective-permute-start
  8.6 1.9 collective-permute-start.1
  10.5 3.6 collective-permute-done.1
  14.2 5.4 concatenate.96
  20.0 3.6 collective-permute-start.2
  24.4 65.2 %all-reduce = f32[128]{0:T(128)S(1)} all-reduce(f32[128]{0:T(128)S(1)} %dynamic-update-slice), channel_id=1, replica_groups=mesh['gx'=8,'gy'=16] {'gx','gy'}, use_global_device_ids=true, to_apply=%add | all-reduce | flops 128 | bytes 1024
  95.3 3.8 fusion.56
  99.4 1.9 copy.7
  101.4 4.0 fusion.54
  113.0 3.0 fusion.391
  117.4 4.7 collective-permute-start.4
  122.0 1.9 collective-permute-start.5
  124.0 3.6 collective-permute-done.5
  127.6 8.3 %concatenate.101 = f32[1084,512]{1,0:T(8,128)} concatenate(f32[30,512]{1,0:T(8,128)S(1)} %collective-permute-done.4, f32[1024,512]{1,0:T(8,128)} %copy-done.9, f32[30,512]{1,0:T(8,128)S(1)} %collective-permute-done.5), dimensions={0} | concatenate | bytes 4440064 | tf_op jit(solution)/shard_map/concatenate | solution.py:23
  137.6 3.1 collective-permute-start.6
  141.5 64.7 %all-reduce.1 = f32[128]{0:T(128)S(1)} all-reduce(f32[128]{0:T(128)S(1)} %dynamic-update-slice.1), channel_id=1, replica_groups=mesh['gx'=8,'gy'=16] {'gx','gy'}, use_global_device_ids=true, to_apply=%add.1 | all-reduce | flops 128 | bytes 1024
  210.5 4.3 fusion.52
  214.9 2.0 copy.11
  216.9 4.5 fusion.50
  225.0 1.9 fusion.107
  228.9 3.0 fusion.388
  233.3 4.0 collective-permute-start.8
  237.3 2.1 collective-permute-start.9
  239.4 3.5 collective-permute-done.9
  242.9 8.3 %concatenate.106 = f32[1084,512]{1,0:T(8,128)} concatenate(f32[30,512]{1,0:T(8,128)S(1)} %collective-permute-done.8, f32[1024,512]{1,0:T(8,128)} %copy-done.3, f32[30,512]{1,0:T(8,128)S(1)} %collective-permute-done.9), dimensions={0} | concatenate | bytes 4440064 | tf_op jit(solution)/shard_map/concatenate | solution.py:23
  252.9 3.7 collective-permute-start.10
  257.3 64.4 %all-reduce.2 = f32[128]{0:T(128)S(1)} all-reduce(f32[128]{0:T(128)S(1)} %dynamic-update-slice.2), channel_id=1, replica_groups=mesh['gx'=8,'gy'=16] {'gx','gy'}, use_global_device_ids=true, to_apply=%add.2 | all-reduce | flops 128 | bytes 1024
  326.0 4.3 fusion.48
  330.4 2.0 copy.15
  332.3 4.5 fusion.46
  344.4 3.0 fusion.385
  348.7 3.9 collective-permute-start.12
  354.6 3.6 collective-permute-done.13
  358.3 8.3 %concatenate.111 = f32[1084,512]{1,0:T(8,128)} concatenate(f32[30,512]{1,0:T(8,128)S(1)} %collective-permute-done.12, f32[1024,512]{1,0:T(8,128)} %copy-done.5, f32[30,512]{1,0:T(8,128)S(1)} %collective-permute-done.13), dimensions={0} | concatenate | bytes 4440064 | tf_op jit(solution)/shard_map/concatenate | solution.py:23
  368.2 3.6 collective-permute-start.14
  372.7 64.9 %all-reduce.3 = f32[128]{0:T(128)S(1)} all-reduce(f32[128]{0:T(128)S(1)} %dynamic-update-slice.3), channel_id=1, replica_groups=mesh['gx'=8,'gy'=16] {'gx','gy'}, use_global_device_ids=true, to_apply=%add.3 | all-reduce | flops 128 | bytes 1024
  441.9 4.3 fusion.44
  446.3 2.0 copy.19
  448.3 4.5 fusion.42
  456.4 1.9 fusion.89
  460.3 3.0 fusion.382
  464.7 3.8 collective-permute-start.16
  468.5 2.1 collective-permute-start.17
  470.6 3.5 collective-permute-done.17
  474.0 8.3 %concatenate.116 = f32[1084,512]{1,0:T(8,128)} concatenate(f32[30,512]{1,0:T(8,128)S(1)} %collective-permute-done.16, f32[1024,512]{1,0:T(8,128)} %copy-done.7, f32[30,512]{1,0:T(8,128)S(1)} %collective-permute-done.17), dimensions={0} | concatenate | bytes 4440064 | tf_op jit(solution)/shard_map/concatenate | solution.py:23
  484.0 3.7 collective-permute-start.18
  488.5 64.6 %all-reduce.4 = f32[128]{0:T(128)S(1)} all-reduce(f32[128]{0:T(128)S(1)} %dynamic-update-slice.4), channel_id=1, replica_groups=mesh['gx'=8,'gy'=16] {'gx','gy'}, use_global_device_ids=true, to_apply=%add.4 | all-reduce | flops 128 | bytes 1024
  557.4 4.3 fusion.40
  561.8 2.0 copy.23
  563.8 4.5 fusion.38
  575.8 3.1 fusion.379
  578.8 3.7 collective-permute-start.20
  582.6 1.9 collective-permute-start.21
  584.5 3.6 collective-permute-done.21
  588.2 5.4 concatenate.121
  594.0 3.4 collective-permute-start.22
  598.2 65.2 %all-reduce.5 = f32[128]{0:T(128)S(1)} all-reduce(f32[128]{0:T(128)S(1)} %dynamic-update-slice.5), channel_id=1, replica_groups=mesh['gx'=8,'gy'=16] {'gx','gy'}, use_global_device_ids=true, to_apply=%add.5 | all-reduce | flops 128 | bytes 1024
  668.4 3.8 fusion.36
  672.8 1.9 copy.27
  674.7 4.0 fusion.34
  682.3 1.9 fusion.71
  684.3 1.9 fusion.124
  686.2 2.9 multiply_add_fusion
  (144 shorter events, 76.9 us)
Async XLA Ops:
  4.1 6.5 copy-start.1
  4.1 6.4 collective-permute-start
  8.6 5.6 collective-permute-start.1
  20.0 74.2 %collective-permute-start.2 = (f32[1084,30]{0,1:T(8,128)S(1)}, f32[1084,30]{0,1:T(8,128)S(1)}, u32[]{:S(2)}, u32[]{:S(2)}) collective-permute-start(f32[1084,30]{0,1:T(8,128)S(1)} %copy.4), channel_id=1, source_target_pairs={{0,1},{1,2},{2,3},{3,4},{4,5},{5,6},{6,7},{7,8},{8,9},{9,10},{10,1... | collective-permute-start | bytes 390248 | tf_op jit(solution)/shard_map/ppermute | solution.py:19
  92.8 6.7 collective-permute-start.3
  107.1 5.8 copy-start.13
  109.1 3.9 copy-start.2
  111.0 2.0 copy-start
  116.0 1.3 copy-start.9
  117.4 6.6 collective-permute-start.4
  122.0 5.6 collective-permute-start.5
  137.6 71.9 %collective-permute-start.6 = (f32[1084,30]{0,1:T(8,128)S(1)}, f32[1084,30]{0,1:T(8,128)S(1)}, u32[]{:S(2)}, u32[]{:S(2)}) collective-permute-start(f32[1084,30]{0,1:T(8,128)S(1)} %copy.8), channel_id=1, source_target_pairs={{0,1},{1,2},{2,3},{3,4},{4,5},{5,6},{6,7},{7,8},{8,9},{9,10},{10,1... | collective-permute-start | bytes 390248 | tf_op jit(solution)/shard_map/ppermute | solution.py:19
  208.2 6.7 collective-permute-start.7
  225.0 3.9 copy-start.17
  226.9 2.0 copy-start.10
  231.9 1.3 copy-start.3
  233.3 6.2 collective-permute-start.8
  237.3 5.6 collective-permute-start.9
  252.9 72.1 %collective-permute-start.10 = (f32[1084,30]{0,1:T(8,128)S(1)}, f32[1084,30]{0,1:T(8,128)S(1)}, u32[]{:S(2)}, u32[]{:S(2)}) collective-permute-start(f32[1084,30]{0,1:T(8,128)S(1)} %copy.12), channel_id=1, source_target_pairs={{0,1},{1,2},{2,3},{3,4},{4,5},{5,6},{6,7},{7,8},{8,9},{9,10},{10,1... | collective-permute-start | bytes 390248 | tf_op jit(solution)/shard_map/ppermute | solution.py:19
  323.7 6.7 collective-permute-start.11
  340.5 3.9 copy-start.14
  342.4 2.0 copy-start.4
  347.4 1.3 copy-start.5
  348.7 5.9 collective-permute-start.12
  352.7 5.6 collective-permute-start.13
  368.2 72.6 %collective-permute-start.14 = (f32[1084,30]{0,1:T(8,128)S(1)}, f32[1084,30]{0,1:T(8,128)S(1)}, u32[]{:S(2)}, u32[]{:S(2)}) collective-permute-start(f32[1084,30]{0,1:T(8,128)S(1)} %copy.16), channel_id=1, source_target_pairs={{0,1},{1,2},{2,3},{3,4},{4,5},{5,6},{6,7},{7,8},{8,9},{9,10},{10,1... | collective-permute-start | bytes 390248 | tf_op jit(solution)/shard_map/ppermute | solution.py:19
  439.6 6.7 collective-permute-start.15
  456.4 3.9 copy-start.15
  458.3 2.0 copy-start.6
  463.3 1.3 copy-start.7
  464.7 5.9 collective-permute-start.16
  468.5 5.6 collective-permute-start.17
  484.0 72.3 %collective-permute-start.18 = (f32[1084,30]{0,1:T(8,128)S(1)}, f32[1084,30]{0,1:T(8,128)S(1)}, u32[]{:S(2)}, u32[]{:S(2)}) collective-permute-start(f32[1084,30]{0,1:T(8,128)S(1)} %copy.20), channel_id=1, source_target_pairs={{0,1},{1,2},{2,3},{3,4},{4,5},{5,6},{6,7},{7,8},{8,9},{9,10},{10,1... | collective-permute-start | bytes 390248 | tf_op jit(solution)/shard_map/ppermute | solution.py:19
  555.1 6.7 collective-permute-start.19
  571.9 3.9 copy-start.16
  573.8 2.0 copy-start.8
  578.8 5.7 copy-start.11
  578.8 5.7 collective-permute-start.20
  582.6 5.6 collective-permute-start.21
  594.0 73.3 %collective-permute-start.22 = (f32[1084,30]{0,1:T(8,128)S(1)}, f32[1084,30]{0,1:T(8,128)S(1)}, u32[]{:S(2)}, u32[]{:S(2)}) collective-permute-start(f32[1084,30]{0,1:T(8,128)S(1)} %copy.24), channel_id=1, source_target_pairs={{0,1},{1,2},{2,3},{3,4},{4,5},{5,6},{6,7},{7,8},{8,9},{9,10},{10,1... | collective-permute-start | bytes 390248 | tf_op jit(solution)/shard_map/ppermute | solution.py:19
  666.0 6.8 collective-permute-start.23
  682.3 3.9 copy-start.18
  684.3 2.0 copy-start.12
where the time goes:
time: 696 us; the launch traced here: 689 us
  blocking collectives  389 us (56%)
  matrix products  101 us (15%)
  local copies, waits for them, and re-layouts  79.1 us (11%)
  starting transfers between devices  65.5 us (9%)
  other arithmetic  22.7 us (3%)
  waiting for transfers between devices  22.4 us (3%)
  between operations  10 us (1%)
    unnamed x6, blocking collectives  389 us
    dot_general x12, matrix products, blur_second(): pieces.append(jnp.dot(window, band, precision=lax.Precision.HIGHEST))  51.2 us
    ppermute x12, starting transfers between devices, padded_2(): lax.ppermute(lax.slice_in_dim(block, block.shape[dim] - width, None, axis...  45.7 us
    dot_general x24, matrix products, blur_first(): pieces.append(jnp.dot(band.T, window, precision=lax.Precision.HIGHEST))  44.5 us
    concatenate x6, local copies, waits for them, and re-layouts, padded_2(): block = jnp.concatenate([low, block, high], axis=dim)  44.1 us
    ppermute x12, waiting for transfers between devices, padded_2(): lax.ppermute(lax.slice_in_dim(block, 0, width, axis=dim), axis, backward)  22.4 us
    ppermute x12, starting transfers between devices, padded_2(): lax.ppermute(lax.slice_in_dim(block, 0, width, axis=dim), axis, backward)  19.8 us
    reduce_sum x6, other arithmetic, per_device(): charge.reshape(rows_local, rows_span, cols_local, cols_span)  18.7 us
  transfers between devices with their start and end apart: 24, of which 8 were waited for; matrix products, arithmetic and copies ran while one was open for 6% of the time, Pallas kernels for 0%

commit v1 on v0

v1 whole, which is shorter than its diff:
```python
import functools
import math

import jax
import jax.numpy as jnp
import numpy as np
from jax import lax
from jax.experimental import pallas as pl
from jax.experimental.pallas import tpu as pltpu
from jax.sharding import PartitionSpec as P

RIM = 30
PAD = 32
COARSE = 1024
FOG = 3072
ITERS = 6
RB = 256
CB = 256
BF = jnp.bfloat16
F32 = jnp.float32
MESH = pl.DeviceIdType.MESH


def two_terms(x):
    hi = np.asarray(x, np.float32).astype(BF)
    lo = (x - hi.astype(np.float64)).astype(np.float32).astype(BF)
    return hi, lo


def taps():
    k = np.arange(-RIM, RIM + 1).astype(np.float64)
    w = np.exp(-k * k / 200.0)
    return w / w.sum()


def band_first():
    w = taps()
    band = np.zeros((RB, RB + 2 * PAD))
    for i in range(RB):
        band[i, i + PAD - RIM : i + PAD + RIM + 1] = w
    hi, lo = two_terms(band)
    return np.concatenate([hi, lo, hi], axis=1)


def band_second():
    w = 0.525 * taps()

    def weight(c, j):
        return w[c - j + RIM] if abs(c - j) <= RIM else 0.0

    main = np.array([[weight(c, j) for j in range(CB)] for c in range(CB)])
    beside = [c for c in range(-PAD, 0)] + [c for c in range(CB, CB + PAD)]
    side = np.array([[weight(c, j) for j in range(CB)] for c in beside])
    mh, ml = two_terms(main)
    sh, sl = two_terms(side)
    return np.concatenate([mh, ml, mh, sh, sh, sl, np.zeros_like(sl)], axis=0)


def fog_matrix(n):
    s = FOG / COARSE
    k = np.arange(n).astype(np.float64)
    spread = k[:, None] - k[None, :]
    return np.exp(-spread * spread / (2.0 * s * s)) / (math.sqrt(2.0 * math.pi) * s)


def split(x):
    hi = x.astype(BF)
    return hi, (x - hi.astype(F32)).astype(BF)


def wide(row):
    return jnp.concatenate([row, row], axis=1)


def kernel(ngx, ngy, cover_hbm, dose_hbm, a1_hbm, w2_hbm, qc_hbm, pc_hbm, out_d, out_r,
           cover, d, f, u, a1, w2, qc, pc, chi, clo, vhi, vlo, vmix, acc, gbuf, fsum,
           rsend, rrecv, csend, crecv, krecv, frs, frr, fcs, fcr, fkr, asend, arecv, bsend, brecv,
           in_sem, out_sem, row_s, row_r, col_s, col_r, cor_s, cor_r,
           frow_s, frow_r, fcol_s, fcol_r, fcor_s, fcor_r, fa_s, fa_r, fb_s, fb_r):
    height, breadth = d.shape
    nb = height // RB
    nt = breadth // CB
    per = COARSE // breadth
    ni, nj = ngx * height // COARSE, ngy * breadth // COARSE
    i, j = lax.axis_index("gx"), lax.axis_index("gy")
    step_x = (lax.rem(i + ngx - 1, ngx), lax.rem(i + 1, ngx))
    step_y = (lax.rem(j + ngy - 1, ngy), lax.rem(j + 1, ngy))
    has_x = (i > 0, i < ngx - 1)
    has_y = (j > 0, j < ngy - 1)
    blk_j = j // per
    side_j = (jnp.maximum(j - 1, 0) // per, jnp.minimum(j + 1, ngy - 1) // per)
    edge = (0, breadth - 128)

    def dev(x, y):
        return {"gx": x, "gy": y}

    def remote(src, dst, ss, rs, to):
        return pltpu.make_async_remote_copy(
            src_ref=src, dst_ref=dst, send_sem=ss, recv_sem=rs, device_id=to, device_id_type=MESH
        )

    def row_copy(v, par):
        return remote(rsend.at[v], rrecv.at[par, 1 - v], row_s.at[v], row_r.at[par, 1 - v],
                      dev(step_x[v], j))

    def row_wait(v, par):
        remote(rsend.at[v], rrecv.at[par, v], row_s.at[v], row_r.at[par, v], dev(step_x[v], j)).wait_recv()

    def col_copy(h, r, par):
        return remote(csend.at[h, r], crecv.at[par, 1 - h, r], col_s.at[h, r],
                      col_r.at[par, 1 - h, r], dev(i, step_y[h]))

    def col_wait(h, r, par):
        remote(csend.at[h, r], crecv.at[par, h, r], col_s.at[h, r], col_r.at[par, h, r],
               dev(i, step_y[h])).wait_recv()

    def cor_copy(v, h, par):
        return remote(rsend.at[v, :, pl.ds(edge[h], 128)], krecv.at[par, 1 - v, 1 - h],
                      cor_s.at[v, h], cor_r.at[par, 1 - v, 1 - h], dev(step_x[v], step_y[h]))

    def cor_wait(v, h, par):
        remote(rsend.at[v, :, pl.ds(edge[h], 128)], krecv.at[par, v, h],
               cor_s.at[v, h], cor_r.at[par, v, h], dev(step_x[v], step_y[h])).wait_recv()

    def frow_copy(v, slot):
        return remote(frs.at[v], frr.at[slot], frow_s.at[v], frow_r.at[slot], dev(step_x[v], j))

    def fcol_copy(h, slot):
        return remote(fcs.at[h], fcr.at[slot], fcol_s.at[h], fcol_r.at[slot], dev(i, step_y[h]))

    def fcor_copy(v, h, sv, sh):
        return remote(frs.at[v, :, pl.ds(edge[h], 128)], fkr.at[sv, sh], fcor_s.at[v, h],
                      fcor_r.at[sv, sh], dev(step_x[v], step_y[h]))

    def share_copy(o, par, slot):
        return remote(asend, arecv.at[par, slot], fa_s.at[o], fa_r.at[par, slot],
                      dev(i, lax.rem(j + o, ngy)))

    def fog_copy(o, par, slot):
        return remote(bsend, brecv.at[par, slot], fb_s.at[o], fb_r.at[par, slot],
                      dev(lax.rem(i + o, ngx), j))

    lane = lax.broadcasted_iota(jnp.int32, (64, 128), 1)
    lane_rb = lax.broadcasted_iota(jnp.int32, (RB, 128), 1)
    lane_pad = lax.broadcasted_iota(jnp.int32, (PAD, 128), 1)
    lane1 = lax.broadcasted_iota(jnp.int32, (1, 128), 1)
    lane_mix = lax.rem(lax.broadcasted_iota(jnp.int32, (RB, 256), 1), 128) < 64

    def roll(x, shift):
        shift = shift % 128
        return x if shift == 0 else pltpu.roll(x, shift, 1)

    def pack(tile, first_lane):
        parts = [roll(tile[64 * q : 64 * q + 64], 32 * q - first_lane) for q in range(4)]
        low = jnp.where(lane < 32, parts[0], parts[1])
        high = jnp.where(lane < 96, parts[2], parts[3])
        return jnp.where(lane < 64, low, high)

    def unpack(piece, first_lane):
        return jnp.concatenate([roll(piece, first_lane - 32 * q) for q in range(4)], axis=0)

    def put_side(rows, c1, c2, left, right, lanes):
        e0 = jnp.where(lanes < 32, left, roll(c2, 32))
        e1 = jnp.where(lanes < 32, roll(c1, 32), right)
        for n, e in enumerate((e0, e1)):
            hi, lo = split(jnp.where(lanes < 64, e, roll(e, 64)))
            cs = slice(breadth + 128 * n, breadth + 128 * n + 128)
            chi[rows, cs] = hi
            if lo is not None:
                clo[rows, cs] = lo

    def first_dot(r, n):
        rows = slice(r * RB, r * RB + RB + 2 * PAD)
        cs = slice(n * CB, n * CB + CB)
        hi = chi[rows, cs]
        return jnp.dot(a1[...], jnp.concatenate([hi, hi, clo[rows, cs]], axis=0),
                       preferred_element_type=F32)

    def first_main(r):
        for n in range(nt):
            hi, lo = split(first_dot(r, n))
            vhi[r * RB : r * RB + RB, n * CB : n * CB + CB] = hi
            vlo[r * RB : r * RB + RB, n * CB : n * CB + CB] = lo

    def put_mix(r, v):
        hi = v.astype(BF).astype(F32)
        vmix[r * RB : r * RB + RB, :] = jnp.where(lane_mix, hi, v - hi).astype(BF)

    def second_dot(r, t):
        rows = slice(r * RB, r * RB + RB)
        hi = vhi[rows, t * CB : t * CB + CB]
        mix = vmix[rows, t * 128 : t * 128 + 128]
        lhs = jnp.concatenate([hi, hi, vlo[rows, t * CB : t * CB + CB], mix, mix], axis=1)
        return jnp.dot(lhs, w2[...], preferred_element_type=F32)

    def send_edges(r, tile, par, wait, start):
        if r == 0 or r == nb - 1:
            v = 0 if r == 0 else 1
            if wait:
                row_copy(v, par).wait_send()
                for h in range(2):
                    cor_copy(v, h, par).wait_send()
            for c0 in range(0, breadth, 128):
                x = tile(c0)
                rsend[v, :, c0 : c0 + 128] = x[:PAD] if v == 0 else x[RB - PAD :]
            if start:
                row_copy(v, par).start()
                for h in range(2):
                    cor_copy(v, h, par).start()
        for h in range(2):
            if wait:
                col_copy(h, r, par).wait_send()
            csend[h, r] = pack(tile(edge[h]), 0 if h == 0 else 96)
            if start:
                col_copy(h, r, par).start()

    def send_share(total, par):
        m = jnp.where(lane1 < 64, jnp.broadcast_to(total, (1, 128)), fsum[...])
        asend[...] = m
        arecv[par, j] = m
        for o in range(1, ngy):
            share_copy(o, par, j).start()

    def reduce_acc():
        return jnp.sum(jnp.sum(acc[...], axis=0, keepdims=True), axis=1, keepdims=True)

    def fold(c):
        return jnp.sum(c.reshape(RB // 8, 8, c.shape[1]), axis=0)

    def row_fog(par):
        for o in range(1, ngy):
            share_copy(o, par, lax.rem(j + o, ngy)).wait_recv()
        total = jnp.zeros((nj, 128), F32)
        before = gbuf[1]
        for s in range(ngy):
            w = jnp.where(lane1 < 64, 1.0, -before[s // per : s // per + 1, :])
            total = total + qc[s] * (arecv[par, s] * w)
        r = total + pltpu.roll(total, 64, 1)
        bsend[...] = r
        brecv[par, i] = r
        for o in range(1, ngx):
            fog_copy(o, par, i).start()

    def get_fog(par):
        for o in range(1, ngx):
            fog_copy(o, par, lax.rem(i + o, ngx)).wait_recv()
        for a in range(3):
            row = jnp.clip(i - 1 + a, 0, ni - 1)
            weight = pc[row]
            total = jnp.zeros((nj, 128), F32)
            for s in range(ngx):
                total = total + weight[s : s + 1, :] * brecv[par, s]
            gbuf[a] = total

    def fog_at(a, col):
        return gbuf[a, pl.ds(col, 1), :]

    def blur_first(par):
        for r in range(1, nb - 1):
            first_main(r)
        get_fog(1 - par)
        halo = []
        for v in range(2):
            row_wait(v, par)
            fog = fog_at(2 * v, blk_j)
            rows = slice(0, PAD) if v == 0 else slice(PAD + height, 2 * PAD + height)
            tiles = []
            for c0 in range(0, breadth, 128):
                x = rrecv[par, v, :, c0 : c0 + 128] - fog * frr[v, :, c0 : c0 + 128]
                x = jnp.where(has_x[v], x, 0.0)
                hi, lo = split(x)
                chi[rows, c0 : c0 + 128] = hi
                clo[rows, c0 : c0 + 128] = lo
                tiles.append(x)
            halo.append(tiles)
        for r in (0, nb - 1):
            first_main(r)
        for v in range(2):
            rows = slice(0, PAD) if v == 0 else slice(PAD + height, 2 * PAD + height)
            sides = []
            for h in range(2):
                cor_wait(v, h, par)
                x = krecv[par, v, h] - fog_at(2 * v, side_j[h]) * fkr[v, h]
                sides.append(roll(jnp.where(has_x[v] & has_y[h], x, 0.0), 32))
            put_side(rows, halo[v][1], halo[v][2], sides[0], sides[1], lane_pad)
        fogs = [fog_at(1, side_j[h]) for h in range(2)]
        for r in range(nb):
            rows = slice(r * RB, r * RB + RB)
            sides = []
            for h in range(2):
                col_wait(h, r, par)
                x = crecv[par, h, r] - fogs[h] * fcr[h, r]
                sides.append(unpack(jnp.where(has_y[h], x, 0.0), 32 * h))
            c1 = f[rows, 128:256] * d[rows, 128:256]
            c2 = f[rows, 256:384] * d[rows, 256:384]
            put_side(slice(PAD + r * RB, PAD + r * RB + RB), c1, c2, sides[0], sides[1], lane_rb)
        for r in range(nb):
            put_mix(r, first_dot(r, nt))

    def advance(k, carry):
        par = lax.rem(k, 2)
        nxt = 1 - par
        blur_first(par)
        own = wide(fog_at(1, blk_j))
        order = [0, nb - 1] + list(range(1, nb - 1))
        for n, r in enumerate(order):
            rows = slice(r * RB, r * RB + RB)
            c = []
            for t in range(nt):
                cs = slice(t * CB, t * CB + CB)
                back = second_dot(r, t)
                now = d[rows, cs] - own
                cov = f[rows, cs]
                new = (now + 0.75) - 0.75 * (cov * now) - back + own * u[rows, cs]
                d[rows, cs] = new
                x = cov * new
                hi, lo = split(x)
                chi[PAD + r * RB : PAD + r * RB + RB, cs] = hi
                clo[PAD + r * RB : PAD + r * RB + RB, cs] = lo
                acc[:, cs] = fold(x) if n == 0 else acc[:, cs] + fold(x)
                c.append(x)
            send_edges(r, lambda c0: c[c0 // CB][:, c0 % CB : c0 % CB + 128], nxt, True, True)
            if n == 1:
                for o in range(1, ngx):
                    fog_copy(o, par, i).wait_send()
                row_fog(par)
        for o in range(1, ngy):
            share_copy(o, par, j).wait_send()
        send_share(reduce_acc(), nxt)
        return carry

    loads = []
    for r in range(nb):
        rows = pl.ds(r * RB, RB)
        loads.append((pltpu.make_async_copy(cover_hbm.at[rows], cover.at[rows], in_sem.at[0, r]),
                      pltpu.make_async_copy(dose_hbm.at[rows], d.at[rows], in_sem.at[1, r])))
    order = [0, nb - 1] + list(range(1, nb - 1))
    for r in order:
        for c in loads[r]:
            c.start()
    consts = [pltpu.make_async_copy(s, t, in_sem.at[2, n])
              for n, (s, t) in enumerate(((a1_hbm, a1), (w2_hbm, w2), (qc_hbm, qc), (pc_hbm, pc)))]
    for c in consts:
        c.start()

    barrier = pltpu.get_barrier_semaphore()
    partners = [dev(i, lax.rem(j + o, ngy)) for o in range(1, ngy)]
    partners += [dev(lax.rem(i + o, ngx), j) for o in range(1, ngx)]
    partners += [dev(x, y) for x in step_x for y in step_y]
    for p in partners:
        pl.semaphore_signal(barrier, inc=1, device_id=p, device_id_type=MESH)

    bsend[...] = jnp.zeros_like(bsend)
    brecv[1, i] = jnp.zeros(bsend.shape, F32)
    chi[0:PAD, :] = jnp.zeros((PAD, chi.shape[1]), BF)
    chi[PAD + height :, :] = jnp.zeros((PAD, chi.shape[1]), BF)

    zero = jnp.zeros((RB, 128), F32)
    for n, r in enumerate(order):
        rows = slice(r * RB, r * RB + RB)
        for c in loads[r]:
            c.wait()
        for t in range(nt):
            cs = slice(t * CB, t * CB + CB)
            cov = cover[rows, cs].astype(F32) * (1.0 / 64.0)
            f[rows, cs] = cov
            x = cov * d[rows, cs]
            acc[:, cs] = fold(x) if n == 0 else acc[:, cs] + fold(x)
            chi[PAD + r * RB : PAD + r * RB + RB, cs] = cov.astype(BF)
        if n == 0:
            pl.semaphore_wait(barrier, len(partners))
        send_edges(r, lambda c0: f[rows, c0 : c0 + 128] * d[rows, c0 : c0 + 128], 0, False, True)
    share = reduce_acc()
    total = jnp.zeros((8, breadth), F32)
    for r in range(nb):
        rows = slice(r * RB, r * RB + RB)
        total = total + fold(f[rows, :])
        for h in range(2):
            fcs[h, r] = pack(f[rows, edge[h] : edge[h] + 128], 0 if h == 0 else 96)
    frs[0] = f[0:PAD, :]
    frs[1] = f[height - PAD :, :]
    fsum[...] = jnp.broadcast_to(
        jnp.sum(jnp.sum(total, axis=0, keepdims=True), axis=1, keepdims=True), (1, 128))
    send_share(share, 0)
    for o in range(1, ngx):
        fog_copy(o, 1, i).start()
    for v in range(2):
        frow_copy(v, 1 - v).start()
        fcol_copy(v, 1 - v).start()
        for h in range(2):
            fcor_copy(v, h, 1 - v, 1 - h).start()

    for c in consts:
        c.wait()
    for r in range(nb):
        rows = slice(PAD + r * RB, PAD + r * RB + RB)
        own_rows = slice(r * RB, r * RB + RB)
        for n, (c0, keep) in enumerate(((256, 1), (128, 0))):
            x = roll(f[own_rows, c0 : c0 + 128], 32)
            e = jnp.where((lane_rb < 32) if keep == 0 else (lane_rb >= 32), x, zero)
            e = jnp.where(lane_rb < 64, e, roll(e, 64))
            chi[rows, breadth + 128 * n : breadth + 128 * n + 128] = e.astype(BF)
    wide_first = 2 * (RB + 2 * PAD)
    for r in range(nb):
        rows = slice(r * RB, r * RB + RB + 2 * PAD)
        for n in range(nt + 1):
            cs = slice(n * CB, n * CB + CB)
            hi = chi[rows, cs]
            v = jnp.dot(a1[:, :wide_first], jnp.concatenate([hi, hi], axis=0), preferred_element_type=F32)
            if n == nt:
                put_mix(r, v)
            else:
                hi, lo = split(v)
                vhi[r * RB : r * RB + RB, cs] = hi
                vlo[r * RB : r * RB + RB, cs] = lo
    for r in range(nb):
        rows = slice(r * RB, r * RB + RB)
        for t in range(nt):
            cs = slice(t * CB, t * CB + CB)
            u[rows, cs] = second_dot(r, t)
    for r in range(nb):
        rows = slice(r * RB, r * RB + RB)
        for t in range(nt):
            cs = slice(t * CB, t * CB + CB)
            hi, lo = split(f[rows, cs] * d[rows, cs])
            chi[PAD + r * RB : PAD + r * RB + RB, cs] = hi
            clo[PAD + r * RB : PAD + r * RB + RB, cs] = lo

    for v in range(2):
        frow_copy(v, v).wait_recv()
        fcol_copy(v, v).wait_recv()
        for h in range(2):
            fcor_copy(v, h, v, h).wait_recv()

    lax.fori_loop(0, ITERS - 1, advance, 0)

    par = (ITERS - 1) % 2
    blur_first(par)
    own = wide(fog_at(1, blk_j))
    for o in range(1, ngx):
        fog_copy(o, par, i).wait_send()
    row_fog(par)
    get_fog(par)
    last = wide(fog_at(1, blk_j))
    stores = []
    for r in range(nb):
        rows = slice(r * RB, r * RB + RB)
        for t in range(nt):
            cs = slice(t * CB, t * CB + CB)
            back = second_dot(r, t)
            now = d[rows, cs] - own
            change = (0.75 - last) - 0.75 * (f[rows, cs] * now) - back + own * u[rows, cs]
            d[rows, cs] = now + change
            u[rows, cs] = change * (1.0 / 1.5)
        for n, (src, dst) in enumerate(((d, out_d), (u, out_r))):
            c = pltpu.make_async_copy(src.at[pl.ds(r * RB, RB)], dst.at[pl.ds(r * RB, RB)], out_sem.at[n, r])
            c.start()
            stores.append(c)
    for v in range(2):
        row_copy(v, par).wait_send()
        frow_copy(v, v).wait_send()
        fcol_copy(v, v).wait_send()
        for h in range(2):
            cor_copy(v, h, par).wait_send()
            fcor_copy(v, h, v, h).wait_send()
        for r in range(nb):
            col_copy(v, r, par).wait_send()
    for o in range(1, ngy):
        share_copy(o, par, j).wait_send()
    for o in range(1, ngx):
        fog_copy(o, par, i).wait_send()
    for c in stores:
        c.wait()


def per_device(ngx, ngy, coverage, dose):
    height, breadth = dose.shape
    nb = height // RB
    ni, nj = ngx * height // COARSE, ngy * breadth // COARSE
    per = COARSE // breadth
    spread_j = fog_matrix(nj) / float(COARSE * COARSE)
    qc = np.stack([np.broadcast_to(spread_j[:, s // per, None], (nj, 128)) for s in range(ngy)])
    pc = np.broadcast_to(0.225 * fog_matrix(ni)[:, :, None], (ni, ni, 128))
    dma = pltpu.SemaphoreType.DMA
    vm = pltpu.VMEM
    wide_cols = breadth + 256
    any_spec = pl.BlockSpec(memory_space=pl.ANY)
    tile = jax.ShapeDtypeStruct((height, breadth), F32)
    return pl.pallas_call(
        functools.partial(kernel, ngx, ngy),
        out_shape=(tile, tile),
        in_specs=[any_spec] * 6,
        out_specs=(any_spec, any_spec),
        scratch_shapes=[
            vm((height, breadth), jnp.int32), vm((height, breadth), F32), vm((height, breadth), F32),
            vm((height, breadth), F32),
            vm((RB, 3 * (RB + 2 * PAD)), BF), vm((4 * CB, CB), BF), vm(qc.shape, F32), vm(pc.shape, F32),
            vm((height + 2 * PAD, wide_cols), BF), vm((height + 2 * PAD, wide_cols), BF),
            vm((height, breadth), BF), vm((height, breadth), BF), vm((height, 256), BF),
            vm((8, breadth), F32), vm((3, nj, 128), F32), vm((1, 128), F32),
            vm((2, PAD, breadth), F32), vm((2, 2, PAD, breadth), F32),
            vm((2, nb, RB // 4, 128), F32), vm((2, 2, nb, RB // 4, 128), F32),
            vm((2, 2, 2, PAD, 128), F32),
            vm((2, PAD, breadth), F32), vm((2, PAD, breadth), F32),
            vm((2, nb, RB // 4, 128), F32), vm((2, nb, RB // 4, 128), F32),
            vm((2, 2, PAD, 128), F32),
            vm((1, 128), F32), vm((2, ngy, 1, 128), F32), vm((nj, 128), F32), vm((2, ngx, nj, 128), F32),
            dma((3, nb)), dma((2, nb)),
            dma((2,)), dma((2, 2)), dma((2, nb)), dma((2, 2, nb)), dma((2, 2)), dma((2, 2, 2)),
            dma((2,)), dma((2,)), dma((2,)), dma((2,)), dma((2, 2)), dma((2, 2)),
            dma((ngy,)), dma((2, ngy)), dma((ngx,)), dma((2, ngx)),
        ],
        compiler_params=pltpu.CompilerParams(
            collective_id=0, has_side_effects=True, vmem_limit_bytes=56 * 2**20
        ),
    )(coverage, dose, jnp.asarray(band_first()), jnp.asarray(band_second()),
      jnp.asarray(qc, F32), jnp.asarray(pc, F32))


def solution(mesh):
    return jax.shard_map(
        functools.partial(per_device, mesh.shape["gx"], mesh.shape["gy"]),
        mesh=mesh,
        in_specs=(P("gx", "gy"), P("gx", "gy")),
        out_specs=(P("gx", "gy"), P("gx", "gy")),
        check_vma=False,
    )
```

time: 696 us -> 80.8 us (0.12)
  blocking collectives: 389 us -> 0 us
  matrix products: 101 us -> 0 us
  Pallas kernels: 0 us -> 75.5 us
  local copies, waits for them, and re-layouts: 79.1 us -> 4.55 us
  starting transfers between devices: 65.5 us -> 0 us
  other arithmetic: 22.7 us -> 0 us
  waiting for transfers between devices: 22.4 us -> 0 us
  between operations: 10 us -> 0.65 us
    unnamed x6 -> x0, blocking collectives: 389 us -> none
    dot_general x42 -> x0, matrix products: 101 us -> none  [the longest x12 51.2 us: blur_second(): pieces.append(jnp.dot(window, band, precision=lax.Precision.HIGHEST))]
    pallas_call x0 -> x1, Pallas kernels: none -> 75.5 us  [per_device(): pl.pallas_call(functools.partial(kernel, ngx, ngy), out_shape=(tile, tile...]
    ppermute x24 -> x0, starting transfers between devices: 65.5 us -> none  [the longest x12 45.7 us: padded_2(): lax.ppermute(lax.slice_in_dim(block, block.shape[dim] - width, None, axis...]
    concatenate x6 -> x0, local copies, waits for them, and re-layouts: 44.1 us -> none  [padded_2(): block = jnp.concatenate([low, block, high], axis=dim)]
    ppermute x24 -> x0, waiting for transfers between devices: 22.4 us -> none  [the longest x12 22.4 us: padded_2(): lax.ppermute(lax.slice_in_dim(block, 0, width, axis=dim), axis, backward)]
    reduce_sum x13 -> x0, other arithmetic: 19.8 us -> none  [the longest x6 18.7 us: per_device(): charge.reshape(rows_local, rows_span, cols_local, cols_span)]
    ppermute x12 -> x0, local copies, waits for them, and re-layouts: 18 us -> none  [the longest x6 11.7 us: padded_2(): lax.ppermute(lax.slice_in_dim(block, 0, width, axis=dim), axis, backward)]
  transfers between devices with their start and end apart: 24 -> 0, of which waited for: 8 -> 0; matrix products, arithmetic and copies ran while one was open for 6% -> 0% of each run, Pallas kernels for 0% -> 0%
where the time goes in v1:
time: 80.8 us; the launch traced here: 80.7 us
  Pallas kernels  75.5 us (93%)
  local copies, waits for them, and re-layouts  4.55 us (6%)
    pallas_call x1, Pallas kernels, per_device(): pl.pallas_call(functools.partial(kernel, ngx, ngy), out_shape=(tile, tile...  75.5 us
    unnamed x4, local copies, waits for them, and re-layouts  4.55 us

profile of v1, /device:TPU:1, one launch (start us, length us, event | category | flops | bytes accessed | tf_op | source)
XLA Modules:
  0.0 80.7 jit_solution(2295908083201904372)
XLA Ops:
  0.6 75.5 %shard_map.77 = (f32[1024,512]{1,0:T(8,128)}, f32[1024,512]{1,0:T(8,128)}) custom-call(s32[1024,512]{1,0:T(8,128)} %cover_hbm.1, f32[1024,512]{1,0:T(8,128)} %dose_hbm.1, bf16[256,960]{1,0:T(8,128)(2,1)} %constant.8.clone.a1_hbm, bf16[1024,256]{1,0:T(8,128)(2,1)} %constant.9.clone.w2_hbm, f32[16,8,128]{2,1,0:T(8,128)} %constant.10.clone.qc_hbm, ...), custom_call_target="tpu_custom_call" | custom-call | tf_op jit(solution)/shard_map/pallas_call | solution.py:489
  76.2 0.0 copy-start
  76.2 3.2 %copy.10 = f32[1024,512]{1,0:T(8,128)} copy(f32[1024,512]{1,0:T(8,128)} %get-tuple-element.4) | data formatting | bytes 4194304
  79.4 0.0 copy-done
  79.4 1.3 %copy.11 = f32[1024,512]{1,0:T(8,128)} copy(f32[1024,512]{1,0:T(8,128)S(1)} %copy-done) | data formatting | bytes 4194304
Async XLA Ops:
  76.2 3.2 %copy-start = (f32[1024,512]{1,0:T(8,128)S(1)}, f32[1024,512]{1,0:T(8,128)}, u32[]{:S(2)}) copy-start(f32[1024,512]{1,0:T(8,128)} %get-tuple-element.5) | copy-start | bytes 6291460

commit v2 on v1

v2 whole, which is shorter than its diff:
```python
import functools
import math

import jax
import jax.numpy as jnp
import numpy as np
from jax import lax
from jax.experimental import pallas as pl
from jax.experimental.pallas import tpu as pltpu
from jax.sharding import PartitionSpec as P

RIM = 30
PAD = 32
COARSE = 1024
FOG = 3072
ITERS = 6
RB = 256
CB = 256
KW = RB + 2 * PAD
BF = jnp.bfloat16
F32 = jnp.float32
MESH = pl.DeviceIdType.MESH


def two_terms(x):
    hi = np.asarray(x, np.float32).astype(BF)
    lo = (x - hi.astype(np.float64)).astype(np.float32).astype(BF)
    return hi, lo


def taps():
    k = np.arange(-RIM, RIM + 1).astype(np.float64)
    w = np.exp(-k * k / 200.0)
    return w / w.sum()


def band_first():
    w = taps()
    band = np.zeros((RB, KW))
    for i in range(RB):
        band[i, i + PAD - RIM : i + PAD + RIM + 1] = w
    hi, lo = two_terms(band)
    return np.concatenate([hi, lo, hi], axis=1)


def band_rows():
    w = taps()
    out = []
    for offset in (-PAD, PAD):
        band = np.array([[w[m + offset - i + RIM] if abs(m + offset - i) <= RIM else 0.0
                          for m in range(PAD)] for i in range(PAD)])
        hi, lo = two_terms(band)
        out.append(np.concatenate([hi, lo, hi, np.zeros_like(hi)], axis=1))
    return np.stack(out)


def second_weights(columns, outputs):
    w = 0.525 * taps()
    return np.array([[w[c - j + RIM] if abs(c - j) <= RIM else 0.0 for j in outputs] for c in columns])


def band_second():
    out = []
    for beside in (range(CB, CB + 128), range(-128, 0)):
        mh, ml = two_terms(second_weights(range(CB), range(CB)))
        xh, xl = two_terms(second_weights(beside, range(CB)))
        out.append(np.concatenate([mh, ml, mh, xh, xl, xh], axis=0))
    return np.stack(out)


def band_halo(breadth):
    columns = list(range(-PAD, 0)) + list(range(breadth, breadth + PAD))
    outputs = list(range(128)) + list(range(breadth - 128, breadth))
    hi, lo = two_terms(second_weights(columns, outputs))
    return np.concatenate([hi, hi, lo, lo], axis=0)


def fog_matrix(n):
    s = FOG / COARSE
    k = np.arange(n).astype(np.float64)
    spread = k[:, None] - k[None, :]
    return np.exp(-spread * spread / (2.0 * s * s)) / (math.sqrt(2.0 * math.pi) * s)


def split(x):
    hi = x.astype(BF)
    return hi, (x - hi.astype(F32)).astype(BF)


def wide(row, n):
    return jnp.concatenate([row] * n, axis=1)


def kernel(ngx, ngy, cover_hbm, dose_hbm, a1_hbm, w2_hbm, wh_hbm, ah_hbm, qc_hbm, pc_hbm, d, out_r,
           cover, f, w, a1, w2, wh, ah, qc, pc, chi, clo, whi, wlo, we, acc, gbuf, fsum, uh,
           rsend, rrecv, csend, crecv, ksend, krecv, frr, fcs, fcr, fks, fkr, fce, fke,
           asend, arecv, bsend, brecv,
           in_sem, row_s, row_r, col_s, col_r, cor_s, cor_r,
           frow_s, frow_r, fcol_s, fcol_r, fcor_s, fcor_r, fa_s, fa_r, fb_s, fb_r):
    height, breadth = d.shape
    nb = height // RB
    nt = breadth // CB
    per = COARSE // breadth
    ni, nj = ngx * height // COARSE, ngy * breadth // COARSE
    i, j = lax.axis_index("gx"), lax.axis_index("gy")
    step_x = (lax.rem(i + ngx - 1, ngx), lax.rem(i + 1, ngx))
    has_x = (i > 0, i < ngx - 1)
    has_y = (j > 0, j < ngy - 1)
    step_y = (jnp.maximum(j - 1, 0), jnp.minimum(j + 1, ngy - 1))
    beside = tuple(jnp.where(has_y[h], i, i + 1 - 2 * lax.rem(i, 2)) for h in range(2))
    into = tuple(jnp.where(has_y[h], 1 - h, h) for h in range(2))
    blk_j = j // per
    side_j = (step_y[0] // per, step_y[1] // per)
    edge = (0, breadth - 128)
    center = slice(128, breadth - 128)
    left, right = slice(0, 128), slice(breadth - 128, breadth)

    def dev(x, y):
        return {"gx": x, "gy": y}

    def remote(src, dst, ss, rs, to):
        return pltpu.make_async_remote_copy(
            src_ref=src, dst_ref=dst, send_sem=ss, recv_sem=rs, device_id=to, device_id_type=MESH
        )

    def row_copy(v, par, slot):
        return remote(rsend.at[v], rrecv.at[par, slot], row_s.at[v], row_r.at[par, slot], dev(step_x[v], j))

    def col_copy(h, r, par, slot):
        return remote(csend.at[h, r], crecv.at[par, slot, r], col_s.at[h, r], col_r.at[par, slot, r],
                      dev(beside[h], step_y[h]))

    def cor_copy(v, h, par, sv, sh):
        return remote(ksend.at[v, h], krecv.at[par, sv, sh], cor_s.at[v, h], cor_r.at[par, sv, sh],
                      dev(step_x[v], step_y[h]))

    def frow_copy(v, slot):
        return remote(f.at[pl.ds(v * (height - PAD), PAD)], frr.at[slot], frow_s.at[v], frow_r.at[slot],
                      dev(step_x[v], j))

    def fcol_copy(h, slot):
        return remote(fcs.at[h], fcr.at[slot], fcol_s.at[h], fcol_r.at[slot], dev(beside[h], step_y[h]))

    def fcor_copy(v, h, sv, sh):
        return remote(fks.at[v, h], fkr.at[sv, sh], fcor_s.at[v, h], fcor_r.at[sv, sh],
                      dev(step_x[v], step_y[h]))

    def share_copy(o, par, slot):
        return remote(asend, arecv.at[par, slot], fa_s.at[o], fa_r.at[par, slot],
                      dev(i, lax.rem(j + o, ngy)))

    def fog_copy(o, par, slot):
        return remote(bsend, brecv.at[par, slot], fb_s.at[o], fb_r.at[par, slot],
                      dev(lax.rem(i + o, ngx), j))

    lane1 = lax.broadcasted_iota(jnp.int32, (1, 128), 1)

    def lanes(n):
        return lax.broadcasted_iota(jnp.int32, (n, 128), 1)

    def roll(x, shift):
        shift = shift % 128
        return x if shift == 0 else pltpu.roll(x, shift, 1)

    def pack(tile, first_lane):
        n = tile.shape[0] // 4
        lane = lanes(n)
        parts = [roll(tile[n * q : n * q + n], 32 * q - first_lane) for q in range(4)]
        low = jnp.where(lane < 32, parts[0], parts[1])
        high = jnp.where(lane < 96, parts[2], parts[3])
        return jnp.where(lane < 64, low, high)

    def unpack(piece, first_lane):
        return jnp.concatenate([roll(piece, first_lane - 32 * q) for q in range(4)], axis=0)

    def mix_ends(low, high):
        lane = lanes(low.shape[0])
        e = jnp.where(lane < 32, low, high)
        e = jnp.where(lane < 64, e, roll(e, 64))
        hi = e.astype(BF).astype(F32)
        return jnp.where(lane < 64, hi, e - hi).astype(BF)

    def put_charge(r, cs, x):
        hi, lo = split(x)
        chi[PAD + r * RB : PAD + r * RB + RB, cs] = hi
        clo[PAD + r * RB : PAD + r * RB + RB, cs] = lo

    def put_blur(rows, cs, x):
        hi, lo = split(x)
        whi[rows, cs] = hi
        wlo[rows, cs] = lo

    def put_main(rows, t, x):
        if t == 0:
            we[rows, 0:128] = x[:, :128]
            put_blur(rows, slice(128, CB), x[:, 128:])
        else:
            put_blur(rows, slice(CB, breadth - 128), x[:, :128])
            we[rows, 128:256] = x[:, 128:]

    def first_dot(r, pick):
        rows = slice(r * RB, r * RB + KW)
        hi = pick(whi, rows)
        return jnp.dot(a1[...], jnp.concatenate([hi, hi, pick(wlo, rows)], axis=0),
                       preferred_element_type=F32)

    def pick_center(ref, rows):
        return ref[rows, center]

    def pick_ends(ref, rows):
        return jnp.concatenate([ref[rows, left], ref[rows, right]], axis=1)

    def second_dot(hi, lo, t):
        own = slice(t * CB, t * CB + CB)
        other = slice(CB, CB + 128) if t == 0 else slice(CB - 128, CB)
        lhs = jnp.concatenate(
            [hi[:, own], hi[:, own], lo[:, own], hi[:, other], hi[:, other], lo[:, other]], axis=1)
        return jnp.dot(lhs, w2[t], preferred_element_type=F32)

    def block_rows(r):
        return slice(PAD + r * RB, PAD + r * RB + RB)

    def fold(x):
        return jnp.sum(x.reshape(x.shape[0] // 8, 8, x.shape[1]), axis=0)

    def add_acc(r, cs, x):
        acc[:, cs] = fold(x) if r == 0 else acc[:, cs] + fold(x)

    def reduce_acc():
        return jnp.sum(jnp.sum(acc[...], axis=0, keepdims=True), axis=1, keepdims=True)

    def fill_edges(r, sides, mids):
        for h in range(2):
            csend[h, r] = pack(sides[h], 96 * h)
        if r == 0 or r == nb - 1:
            v = 0 if r == 0 else 1
            part = slice(0, PAD) if v == 0 else slice(RB - PAD, RB)
            rsend[v, :, left] = sides[0][part]
            rsend[v, :, right] = sides[1][part]
            rsend[v, :, center] = mids[part]
            for h in range(2):
                ksend[v, h] = pack(sides[h][part], 96 * h)

    def start_edges(r, par):
        for h in range(2):
            col_copy(h, r, par, into[h]).start()
        if r == 0 or r == nb - 1:
            v = 0 if r == 0 else 1
            row_copy(v, par, 1 - v).start()
            for h in range(2):
                cor_copy(v, h, par, 1 - v, into[h]).start()

    def sent_edges(r):
        for h in range(2):
            col_copy(h, r, 0, h).wait_send()
        if r == 0 or r == nb - 1:
            v = 0 if r == 0 else 1
            row_copy(v, 0, v).wait_send()
            for h in range(2):
                cor_copy(v, h, 0, v, h).wait_send()

    def send_share(total, par):
        m = jnp.where(lane1 < 64, jnp.broadcast_to(total, (1, 128)), fsum[...])
        asend[...] = m
        arecv[par, j] = m
        for o in range(1, ngy):
            share_copy(o, par, j).start()

    def row_fog(par):
        for o in range(1, ngy):
            share_copy(o, par, lax.rem(j + o, ngy)).wait_recv()
        total = jnp.zeros((nj, 128), F32)
        before = gbuf[1]
        for s in range(ngy):
            m = jnp.where(lane1 < 64, 1.0, -before[s // per : s // per + 1, :])
            total = total + qc[s] * (arecv[par, s] * m)
        r = total + pltpu.roll(total, 64, 1)
        bsend[...] = r
        brecv[par, i] = r
        for o in range(1, ngx):
            fog_copy(o, par, i).start()

    def get_fog(par):
        for o in range(1, ngx):
            fog_copy(o, par, lax.rem(i + o, ngx)).wait_recv()
        for a in range(3):
            row = jnp.clip(i - 1 + a, 0, ni - 1)
            weight = pc[row]
            total = jnp.zeros((nj, 128), F32)
            for s in range(ngx):
                total = total + weight[s : s + 1, :] * brecv[par, s]
            gbuf[a] = total

    def fog_at(a, col):
        return gbuf[a, pl.ds(col, 1), :]

    def blur_inner(par, last):
        def block(r):
            rows = slice(r * RB, r * RB + RB)
            now = d[rows, center]
            change = 0.75 - 0.75 * (f[rows, center] * now) - first_dot(r, pick_center)
            if last:
                out_r[rows, center] = change
            else:
                d[rows, center] = now + change

        for r in range(nb):
            rows = block_rows(r)
            for t in range(nt):
                put_main(rows, t, second_dot(chi[rows, :], clo[rows, :], t))
        for r in range(1, nb - 1):
            block(r)
        halo = []
        for v in range(2):
            row_copy(v, par, v).wait_recv()
        for v in range(2):
            halo.append(split(jnp.where(has_x[v], rrecv[par, v], 0.0)))
        hi = jnp.concatenate([halo[0][0], halo[1][0]], axis=0)
        lo = jnp.concatenate([halo[0][1], halo[1][1]], axis=0)
        for t in range(nt):
            x = second_dot(hi, lo, t)
            put_main(slice(0, PAD), t, x[:PAD])
            put_main(slice(PAD + height, 2 * PAD + height), t, x[PAD:])
        for r in (0, nb - 1):
            block(r)

    def fog_rows(r, x, cs):
        n = (cs.stop - cs.start) // 128
        if r == 0:
            first = x[:PAD] + wide(fog_at(0, blk_j), n) * uh[0, :, cs]
            return jnp.concatenate([first, x[PAD:]], axis=0)
        if r == nb - 1:
            final = x[RB - PAD :] + wide(fog_at(2, blk_j), n) * uh[1, :, cs]
            return jnp.concatenate([x[: RB - PAD], final], axis=0)
        return x

    def get_corners(v, par):
        sides = []
        for h in range(2):
            x = krecv[par, v, h] - fog_at(2 * v, side_j[h]) * fke[v, h]
            sides.append(unpack(jnp.where(has_x[v] & has_y[h], x, 0.0), 32 * h))
        return mix_ends(sides[0], sides[1])

    def get_columns(r, par):
        sides = []
        for h in range(2):
            x = crecv[par, h, r] - fog_at(1, side_j[h]) * fce[h, r]
            sides.append(unpack(jnp.where(has_y[h], x, 0.0), 32 * h))
        return mix_ends(sides[0], sides[1])

    def put_ends(first, mix):
        rows = slice(first, first + mix.shape[0])
        x = we[rows, :] + jnp.dot(jnp.concatenate([mix, mix], axis=1), wh[...], preferred_element_type=F32)
        put_blur(rows, left, x[:, :128])
        put_blur(rows, right, x[:, 128:])

    def blur_ends(par, use):
        half = nb // 2
        for h in range(2):
            cor_copy(0, h, par, 0, h).wait_recv()
            for r in range(half + 1):
                col_copy(h, r, par, h).wait_recv()
        for r in range(nb):
            sent_edges(r)
        put_ends(0, jnp.concatenate(
            [get_corners(0, par)] + [get_columns(r, par) for r in range(half + 1)], axis=0))
        use([(r, first_dot(r, pick_ends)) for r in range(half)])
        for h in range(2):
            cor_copy(1, h, par, 1, h).wait_recv()
            for r in range(half + 1, nb):
                col_copy(h, r, par, h).wait_recv()
        put_ends(PAD + (half + 1) * RB, jnp.concatenate(
            [get_columns(r, par) for r in range(half + 1, nb)] + [get_corners(1, par)], axis=0))
        use([(r, first_dot(r, pick_ends)) for r in range(half, nb)])

    def advance(k, carry):
        par = lax.rem(k, 2)
        nxt = 1 - par
        blur_inner(par, False)
        get_fog(1 - par)

        @pl.when(k == 1)
        def _():
            own_halo_coverage()

        own = fog_at(1, blk_j)
        for r in range(nb):
            rows = slice(r * RB, r * RB + RB)
            new = d[rows, center] + wide(own, (breadth - 256) // 128) * w[rows, center]
            new = fog_rows(r, new, center)
            d[rows, center] = new
            x = f[rows, center] * new
            put_charge(r, center, x)
            add_acc(r, center, x)

        def use(backs):
            for r, back in backs:
                rows = slice(r * RB, r * RB + RB)
                sides = []
                for h in range(2):
                    cs = slice(edge[h], edge[h] + 128)
                    now = d[rows, cs]
                    cov = f[rows, cs]
                    new = now + (0.75 - 0.75 * (cov * now) - back[:, 128 * h : 128 * h + 128])
                    new = fog_rows(r, new + own * w[rows, cs], cs)
                    d[rows, cs] = new
                    x = cov * new
                    put_charge(r, cs, x)
                    add_acc(r, cs, x)
                    sides.append(x)
                fill_edges(r, sides, f[rows, center] * d[rows, center])
            for r, _ in backs:
                start_edges(r, nxt)

        blur_ends(par, use)
        for o in range(1, ngx):
            fog_copy(o, par, i).wait_send()
        row_fog(par)
        for o in range(1, ngy):
            share_copy(o, par, j).wait_send()
        send_share(reduce_acc(), nxt)
        return carry

    def own_halo_coverage():
        for v in range(2):
            frow_copy(v, v).wait_recv()
            fcol_copy(v, v).wait_recv()
            for h in range(2):
                fcor_copy(v, h, v, h).wait_recv()
        fce[...] = fcr[...]
        fke[...] = fkr[...]
        halo = jnp.concatenate([jnp.where(has_x[v], frr[v], 0.0) for v in range(2)], axis=0).astype(BF)
        for t in range(nt):
            hi, lo = split(second_dot(halo, jnp.zeros_like(halo), t))
            for v in range(2):
                part = slice(v * PAD, v * PAD + PAD)
                terms = jnp.concatenate([hi[part], hi[part], lo[part], jnp.zeros((PAD, CB), BF)], axis=0)
                uh[v, :, t * CB : t * CB + CB] = jnp.dot(ah[v], terms, preferred_element_type=F32)

    loads = []
    for r in range(nb):
        rows = pl.ds(r * RB, RB)
        loads.append((pltpu.make_async_copy(cover_hbm.at[rows], cover.at[rows], in_sem.at[0, r]),
                      pltpu.make_async_copy(dose_hbm.at[rows], d.at[rows], in_sem.at[1, r])))
        for c in loads[r]:
            c.start()
    pairs = ((a1_hbm, a1), (w2_hbm, w2), (wh_hbm, wh), (ah_hbm, ah), (qc_hbm, qc), (pc_hbm, pc))
    consts = [pltpu.make_async_copy(s, t, in_sem.at[2, n]) for n, (s, t) in enumerate(pairs)]
    for c in consts:
        c.start()

    barrier = pltpu.get_barrier_semaphore()
    partners = [dev(step_x[v], step_y[h]) for v in range(2) for h in range(2)]
    partners += [dev(i, lax.rem(j + o, ngy)) for o in range(1, ngy)]
    partners += [dev(lax.rem(i + o, ngx), j) for o in range(1, ngx)]
    for p in partners:
        pl.semaphore_signal(barrier, inc=1, device_id=p, device_id_type=MESH)

    bsend[...] = jnp.zeros_like(bsend)
    brecv[1, i] = jnp.zeros(bsend.shape, F32)
    uh[...] = jnp.zeros_like(uh)
    fce[...] = jnp.zeros_like(fce)
    fke[...] = jnp.zeros_like(fke)
    clo[...] = jnp.zeros_like(clo)
    for ref in (whi, wlo):
        ref[0:PAD, :] = jnp.zeros((PAD, breadth), BF)
        ref[PAD + height :, :] = jnp.zeros((PAD, breadth), BF)

    total = jnp.zeros((8, breadth), F32)
    for r in range(nb):
        rows = slice(r * RB, r * RB + RB)
        for c in loads[r]:
            c.wait()
        cov = cover[rows, :].astype(F32) * (1.0 / 64.0)
        f[rows, :] = cov
        total = total + fold(cov)
        chi[PAD + r * RB : PAD + r * RB + RB, :] = cov.astype(BF)
        for h in range(2):
            fcs[h, r] = pack(cov[:, edge[h] : edge[h] + 128], 96 * h)
            if r == 0:
                fks[0, h] = pack(cov[:PAD, edge[h] : edge[h] + 128], 96 * h)
            if r == nb - 1:
                fks[1, h] = pack(cov[RB - PAD :, edge[h] : edge[h] + 128], 96 * h)
        x = cov * d[rows, :]
        add_acc(r, slice(0, breadth), x)
        fill_edges(r, (x[:, left], x[:, right]), x[:, center])
    fsum[...] = jnp.broadcast_to(
        jnp.sum(jnp.sum(total, axis=0, keepdims=True), axis=1, keepdims=True), (1, 128))
    share = reduce_acc()

    for c in consts:
        c.wait()
    for r in range(nb):
        rows = block_rows(r)
        for t in range(nt):
            put_blur(rows, slice(t * CB, t * CB + CB), second_dot(chi[rows, :], clo[rows, :], t))
    for r in range(nb):
        rows = slice(r * RB, r * RB + RB)
        for t in range(nt):
            cs = slice(t * CB, t * CB + CB)
            u = first_dot(r, lambda ref, win: ref[win, cs])
            w[rows, cs] = u + 0.75 * f[rows, cs] - 1.0

    pl.semaphore_wait(barrier, len(partners))
    for r in range(nb):
        start_edges(r, 0)
    send_share(share, 0)
    for o in range(1, ngx):
        fog_copy(o, 1, i).start()
    for v in range(2):
        frow_copy(v, 1 - v).start()
        fcol_copy(v, into[v]).start()
        for h in range(2):
            fcor_copy(v, h, 1 - v, into[h]).start()
    for r in range(nb):
        rows = slice(r * RB, r * RB + RB)
        put_charge(r, slice(0, breadth), f[rows, :] * d[rows, :])

    lax.fori_loop(0, ITERS - 1, advance, 0)

    par = (ITERS - 1) % 2
    blur_inner(par, True)
    get_fog(1 - par)
    own = fog_at(1, blk_j)
    for r in range(nb):
        rows = slice(r * RB, r * RB + RB)
        now = d[rows, center] - wide(own, (breadth - 256) // 128)
        change = out_r[rows, center] + wide(own, (breadth - 256) // 128) * (w[rows, center] + 1.0)
        change = fog_rows(r, change, center)
        d[rows, center] = now
        out_r[rows, center] = change

    def use_last(backs):
        for r, back in backs:
            rows = slice(r * RB, r * RB + RB)
            for h in range(2):
                cs = slice(edge[h], edge[h] + 128)
                now = d[rows, cs]
                change = 0.75 - 0.75 * (f[rows, cs] * now) - back[:, 128 * h : 128 * h + 128]
                change = change + own * (w[rows, cs] + 1.0)
                d[rows, cs] = now - own
                out_r[rows, cs] = fog_rows(r, change, cs)

    blur_ends(par, use_last)
    for o in range(1, ngx):
        fog_copy(o, par, i).wait_send()
    row_fog(par)
    get_fog(par)
    last = wide(fog_at(1, blk_j), breadth // 128)
    for r in range(nb):
        rows = slice(r * RB, r * RB + RB)
        change = out_r[rows, :] - last
        d[rows, :] = d[rows, :] + change
        out_r[rows, :] = change * (1.0 / 1.5)
    for v in range(2):
        frow_copy(v, v).wait_send()
        fcol_copy(v, v).wait_send()
        for h in range(2):
            fcor_copy(v, h, v, h).wait_send()
    for o in range(1, ngy):
        share_copy(o, par, j).wait_send()
    for o in range(1, ngx):
        fog_copy(o, par, i).wait_send()


def per_device(ngx, ngy, coverage, dose):
    height, breadth = dose.shape
    nb = height // RB
    ni, nj = ngx * height // COARSE, ngy * breadth // COARSE
    per = COARSE // breadth
    spread_j = fog_matrix(nj) / float(COARSE * COARSE)
    qc = np.stack([np.broadcast_to(spread_j[:, s // per, None], (nj, 128)) for s in range(ngy)])
    pc = np.broadcast_to(0.225 * fog_matrix(ni)[:, :, None], (ni, ni, 128))
    a1, w2, wh, ah = band_first(), band_second(), band_halo(breadth), band_rows()
    dma = pltpu.SemaphoreType.DMA
    vm = pltpu.VMEM
    any_spec = pl.BlockSpec(memory_space=pl.ANY)
    tile, padded = (height, breadth), (height + 2 * PAD, breadth)
    rows, cols, corners = (2, PAD, breadth), (2, nb, RB // 4, 128), (2, 2, PAD // 4, 128)
    return pl.pallas_call(
        functools.partial(kernel, ngx, ngy),
        out_shape=(vm(tile, F32), vm(tile, F32)),
        in_specs=[any_spec] * 8,
        out_specs=(pl.BlockSpec(memory_space=vm), pl.BlockSpec(memory_space=vm)),
        scratch_shapes=[
            vm(tile, jnp.int32), vm(tile, F32), vm(tile, F32),
            vm(a1.shape, BF), vm(w2.shape, BF), vm(wh.shape, BF), vm(ah.shape, BF), vm(qc.shape, F32), vm(pc.shape, F32),
            vm(padded, BF), vm(padded, BF), vm(padded, BF), vm(padded, BF), vm((height + 2 * PAD, 256), F32),
            vm((8, breadth), F32), vm((3, nj, 128), F32), vm((1, 128), F32), vm(rows, F32),
            vm(rows, F32), vm((2,) + rows, F32), vm(cols, F32), vm((2,) + cols, F32),
            vm(corners, F32), vm((2,) + corners, F32),
            vm(rows, F32), vm(cols, F32), vm(cols, F32), vm(corners, F32), vm(corners, F32),
            vm(cols, F32), vm(corners, F32),
            vm((1, 128), F32), vm((2, ngy, 1, 128), F32), vm((nj, 128), F32), vm((2, ngx, nj, 128), F32),
            dma((3, max(nb, 6))),
            dma((2,)), dma((2, 2)), dma((2, nb)), dma((2, 2, nb)), dma((2, 2)), dma((2, 2, 2)),
            dma((2,)), dma((2,)), dma((2,)), dma((2,)), dma((2, 2)), dma((2, 2)),
            dma((ngy,)), dma((2, ngy)), dma((ngx,)), dma((2, ngx)),
        ],
        compiler_params=pltpu.CompilerParams(
            collective_id=0, has_side_effects=True, vmem_limit_bytes=40 * 2**20
        ),
    )(coverage, dose, jnp.asarray(a1), jnp.asarray(w2), jnp.asarray(wh), jnp.asarray(ah),
      jnp.asarray(qc, F32), jnp.asarray(pc, F32))


def solution(mesh):
    return jax.shard_map(
        functools.partial(per_device, mesh.shape["gx"], mesh.shape["gy"]),
        mesh=mesh,
        in_specs=(P("gx", "gy"), P("gx", "gy")),
        out_specs=(P("gx", "gy"), P("gx", "gy")),
        check_vma=False,
    )
```

time: 80.8 us -> 71.8 us (0.89)
  Pallas kernels: 75.5 us -> 59.3 us
  local copies, waits for them, and re-layouts: 4.55 us -> 11.3 us
    pallas_call x1, Pallas kernels: 75.5 us -> 59.3 us  [per_device(): pl.pallas_call(functools.partial(kernel, ngx, ngy), out_shape=(vm(tile, F...]
    unnamed x4 -> x18, local copies, waits for them, and re-layouts: 4.55 us -> 11.3 us
where the time goes in v2:
time: 71.8 us; the launch traced here: 71.3 us
  Pallas kernels  59.3 us (83%)
  local copies, waits for them, and re-layouts  11.3 us (16%)
    pallas_call x1, Pallas kernels, per_device(): pl.pallas_call(functools.partial(kernel, ngx, ngy), out_shape=(vm(tile, F...  59.3 us
    unnamed x18, local copies, waits for them, and re-layouts  11.3 us

profile of v2, /device:TPU:1, one launch (start us, length us, event | category | flops | bytes accessed | tf_op | source)
XLA Modules:
  0.0 71.3 jit_solution(5204684714020200076)
XLA Ops:
  0.6 0.0 copy-start
  0.6 1.6 %copy-done = s32[1024,512]{1,0:T(8,128)S(1)} copy-done((s32[1024,512]{1,0:T(8,128)S(1)}, s32[1024,512]{1,0:T(8,128)}, u32[]{:S(2)}) %copy-start) | copy-done | bytes 2097176
  2.2 0.0 copy-start.1
  2.2 1.6 %copy-done.1 = f32[1024,512]{1,0:T(8,128)S(1)} copy-done((f32[1024,512]{1,0:T(8,128)S(1)}, f32[1024,512]{1,0:T(8,128)}, u32[]{:S(2)}) %copy-start.1) | copy-done | bytes 2097176
  3.8 0.0 copy-start.2
  3.8 1.3 %copy-done.2 = bf16[2,1152,256]{2,1,0:T(8,128)(2,1)S(1)} copy-done((bf16[2,1152,256]{2,1,0:T(8,128)(2,1)S(1)}, bf16[2,1152,256]{2,1,0:T(8,128)(2,1)}, u32[]{:S(2)}) %copy-start.2) | copy-done | bytes 1179672
  5.1 0.0 copy-start.3
  5.1 1.0 %copy-done.3 = bf16[256,960]{1,0:T(8,128)(2,1)S(1)} copy-done((bf16[256,960]{1,0:T(8,128)(2,1)S(1)}, bf16[256,960]{1,0:T(8,128)(2,1)}, u32[]{:S(2)}) %copy-start.3) | copy-done | bytes 491544
  6.1 0.0 copy-start.4
  6.1 0.9 %copy-done.4 = bf16[256,256]{1,0:T(8,128)(2,1)S(1)} copy-done((bf16[256,256]{1,0:T(8,128)(2,1)S(1)}, bf16[256,256]{1,0:T(8,128)(2,1)}, u32[]{:S(2)}) %copy-start.4) | copy-done | bytes 131096
  7.0 0.0 copy-start.5
  7.0 0.8 %copy-done.5 = f32[16,8,128]{2,1,0:T(8,128)S(1)} copy-done((f32[16,8,128]{2,1,0:T(8,128)S(1)}, f32[16,8,128]{2,1,0:T(8,128)}, u32[]{:S(2)}) %copy-start.5) | copy-done | bytes 65560
  7.9 0.0 copy-start.6
  7.9 0.8 %copy-done.6 = f32[8,8,128]{2,1,0:T(8,128)S(1)} copy-done((f32[8,8,128]{2,1,0:T(8,128)S(1)}, f32[8,8,128]{2,1,0:T(8,128)}, u32[]{:S(2)}) %copy-start.6) | copy-done | bytes 32792
  8.6 0.0 copy-start.7
  8.6 0.7 %copy-done.7 = bf16[2,32,128]{2,1,0:T(8,128)(2,1)S(1)} copy-done((bf16[2,32,128]{2,1,0:T(8,128)(2,1)S(1)}, bf16[2,32,128]{2,1,0:T(8,128)(2,1)}, u32[]{:S(2)}) %copy-start.7) | copy-done | bytes 16408
  9.3 59.3 %shard_map.95 = (f32[1024,512]{1,0:T(8,128)S(1)}, f32[1024,512]{1,0:T(8,128)S(1)}) custom-call(s32[1024,512]{1,0:T(8,128)S(1)} %copy-done, f32[1024,512]{1,0:T(8,128)S(1)} %copy-done.1, bf16[256,960]{1,0:T(8,128)(2,1)S(1)} %copy-done.3, bf16[2,1152,256]{2,1,0:T(8,128)(2,1)S(1)} %copy-done.2, bf16[256,256]{1,0:T(8,128)(2,1)S(1)} %copy-done.4, ...), custom_call_target="tpu_custom_call" | custom-call | tf_op jit(solution)/shard_map/pallas_call | solution.py:580
  68.7 1.3 %copy.12 = f32[1024,512]{1,0:T(8,128)} copy(f32[1024,512]{1,0:T(8,128)S(1)} %get-tuple-element.2) | data formatting | bytes 4194304
  70.0 1.3 %copy.13 = f32[1024,512]{1,0:T(8,128)} copy(f32[1024,512]{1,0:T(8,128)S(1)} %get-tuple-element.3) | data formatting | bytes 4194304
Async XLA Ops:
  0.6 1.6 %copy-start = (s32[1024,512]{1,0:T(8,128)S(1)}, s32[1024,512]{1,0:T(8,128)}, u32[]{:S(2)}) copy-start(s32[1024,512]{1,0:T(8,128)} %cover_hbm.1) | copy-start | bytes 6291460
  2.2 1.6 %copy-start.1 = (f32[1024,512]{1,0:T(8,128)S(1)}, f32[1024,512]{1,0:T(8,128)}, u32[]{:S(2)}) copy-start(f32[1024,512]{1,0:T(8,128)} %dose_hbm.1) | copy-start | bytes 6291460
  3.8 1.3 %copy-start.2 = (bf16[2,1152,256]{2,1,0:T(8,128)(2,1)S(1)}, bf16[2,1152,256]{2,1,0:T(8,128)(2,1)}, u32[]{:S(2)}) copy-start(bf16[2,1152,256]{2,1,0:T(8,128)(2,1)} %constant.13.clone.w2_hbm) | copy-start | bytes 3538948
  5.1 1.0 %copy-start.3 = (bf16[256,960]{1,0:T(8,128)(2,1)S(1)}, bf16[256,960]{1,0:T(8,128)(2,1)}, u32[]{:S(2)}) copy-start(bf16[256,960]{1,0:T(8,128)(2,1)} %constant.12.clone.a1_hbm) | copy-start | bytes 1474564
  6.1 0.9 %copy-start.4 = (bf16[256,256]{1,0:T(8,128)(2,1)S(1)}, bf16[256,256]{1,0:T(8,128)(2,1)}, u32[]{:S(2)}) copy-start(bf16[256,256]{1,0:T(8,128)(2,1)} %constant.14.clone.wh_hbm) | copy-start | bytes 393220
  7.0 0.8 %copy-start.5 = (f32[16,8,128]{2,1,0:T(8,128)S(1)}, f32[16,8,128]{2,1,0:T(8,128)}, u32[]{:S(2)}) copy-start(f32[16,8,128]{2,1,0:T(8,128)} %constant.16.clone.qc_hbm) | copy-start | bytes 196612
  7.9 0.8 %copy-start.6 = (f32[8,8,128]{2,1,0:T(8,128)S(1)}, f32[8,8,128]{2,1,0:T(8,128)}, u32[]{:S(2)}) copy-start(f32[8,8,128]{2,1,0:T(8,128)} %constant.17.clone.pc_hbm) | copy-start | bytes 98308
  8.6 0.7 %copy-start.7 = (bf16[2,32,128]{2,1,0:T(8,128)(2,1)S(1)}, bf16[2,32,128]{2,1,0:T(8,128)(2,1)}, u32[]{:S(2)}) copy-start(bf16[2,32,128]{2,1,0:T(8,128)(2,1)} %constant.15.clone.ah_hbm) | copy-start | bytes 49156

commit v3 on v2

--- a/solution.py
+++ b/solution.py
@@ -362,26 +362,24 @@
                 col_copy(h, r, par, h).wait_recv()
         for r in range(nb):
             sent_edges(r)
-        put_ends(0, jnp.concatenate(
-            [get_corners(0, par)] + [get_columns(r, par) for r in range(half + 1)], axis=0))
+        put_ends(0, get_corners(0, par))
+        for r in range(half + 1):
+            put_ends(PAD + r * RB, get_columns(r, par))
         use([(r, first_dot(r, pick_ends)) for r in range(half)])
         for h in range(2):
             cor_copy(1, h, par, 1, h).wait_recv()
             for r in range(half + 1, nb):
                 col_copy(h, r, par, h).wait_recv()
-        put_ends(PAD + (half + 1) * RB, jnp.concatenate(
-            [get_columns(r, par) for r in range(half + 1, nb)] + [get_corners(1, par)], axis=0))
+        for r in range(half + 1, nb):
+            put_ends(PAD + r * RB, get_columns(r, par))
+        put_ends(PAD + height, get_corners(1, par))
         use([(r, first_dot(r, pick_ends)) for r in range(half, nb)])
 
     def advance(k, carry):
-        par = lax.rem(k, 2)
+        par = k % 2 if isinstance(k, int) else lax.rem(k, 2)
         nxt = 1 - par
         blur_inner(par, False)
         get_fog(1 - par)
-
-        @pl.when(k == 1)
-        def _():
-            own_halo_coverage()
 
         own = fog_at(1, blk_j)
         for r in range(nb):
@@ -516,7 +514,9 @@
         rows = slice(r * RB, r * RB + RB)
         put_charge(r, slice(0, breadth), f[rows, :] * d[rows, :])
 
-    lax.fori_loop(0, ITERS - 1, advance, 0)
+    advance(0, 0)
+    own_halo_coverage()
+    lax.fori_loop(1, ITERS - 1, advance, 0)
 
     par = (ITERS - 1) % 2
     blur_inner(par, True)
@@ -574,7 +574,7 @@
     a1, w2, wh, ah = band_first(), band_second(), band_halo(breadth), band_rows()
     dma = pltpu.SemaphoreType.DMA
     vm = pltpu.VMEM
-    any_spec = pl.BlockSpec(memory_space=pl.ANY)
+    any_spec = pl.BlockSpec(memory_space=pltpu.HBM)
     tile, padded = (height, breadth), (height + 2 * PAD, breadth)
     rows, cols, corners = (2, PAD, breadth), (2, nb, RB // 4, 128), (2, 2, PAD // 4, 128)
     return pl.pallas_call(
@@ -598,7 +598,7 @@
             dma((ngy,)), dma((2, ngy)), dma((ngx,)), dma((2, ngx)),
         ],
         compiler_params=pltpu.CompilerParams(
-            collective_id=0, has_side_effects=True, vmem_limit_bytes=40 * 2**20
+            collective_id=0, has_side_effects=True, vmem_limit_bytes=52 * 2**20
         ),
     )(coverage, dose, jnp.asarray(a1), jnp.asarray(w2), jnp.asarray(wh), jnp.asarray(ah),
       jnp.asarray(qc, F32), jnp.asarray(pc, F32))

time: 71.8 us -> 62.5 us (0.87)
  local copies, waits for them, and re-layouts: 11.3 us -> 2.64 us
    unnamed x18 -> x2, local copies, waits for them, and re-layouts: 11.3 us -> 2.64 us
where the time goes in v3:
time: 62.5 us; the launch traced here: 62.4 us
  Pallas kernels  59.1 us (95%)
  local copies, waits for them, and re-layouts  2.64 us (4%)
  between operations  0.64 us (1%)
    pallas_call x1, Pallas kernels, per_device(): pl.pallas_call(functools.partial(kernel, ngx, ngy), out_shape=(vm(tile, F...  59.1 us
    unnamed x2, local copies, waits for them, and re-layouts  2.64 us

profile of v3, /device:TPU:1, one launch (start us, length us, event | category | flops | bytes accessed | tf_op | source)
XLA Modules:
  0.0 62.4 jit_solution(14047169270047440515)
XLA Ops:
  0.6 59.1 %shard_map.95 = (f32[1024,512]{1,0:T(8,128)S(1)}, f32[1024,512]{1,0:T(8,128)S(1)}) custom-call(s32[1024,512]{1,0:T(8,128)} %cover_hbm.1, f32[1024,512]{1,0:T(8,128)} %dose_hbm.1, bf16[256,960]{1,0:T(8,128)(2,1)} %constant.12.clone.a1_hbm, bf16[2,1152,256]{2,1,0:T(8,128)(2,1)} %constant.13.clone.w2_hbm, bf16[256,256]{1,0:T(8,128)(2,1)} %constant.14.clone.wh_hbm, ...), custom_call_target="tpu_custom_call" | custom-call | tf_op jit(solution)/shard_map/pallas_call | solution.py:580
  59.8 1.3 %copy.12 = f32[1024,512]{1,0:T(8,128)} copy(f32[1024,512]{1,0:T(8,128)S(1)} %get-tuple-element.2) | data formatting | bytes 4194304
  61.1 1.3 %copy.13 = f32[1024,512]{1,0:T(8,128)} copy(f32[1024,512]{1,0:T(8,128)S(1)} %get-tuple-element.3) | data formatting | bytes 4194304

commit v4 on v3

--- a/solution.py
+++ b/solution.py
@@ -91,7 +91,7 @@
     return jnp.concatenate([row] * n, axis=1)
 
 
-def kernel(ngx, ngy, cover_hbm, dose_hbm, a1_hbm, w2_hbm, wh_hbm, ah_hbm, qc_hbm, pc_hbm, d, out_r,
+def kernel(ngx, ngy, cover_hbm, dose_hbm, a1_hbm, w2_hbm, wh_hbm, ah_hbm, qc_hbm, pc_hbm, d, out_r, out_g,
            cover, f, w, a1, w2, wh, ah, qc, pc, chi, clo, whi, wlo, we, acc, gbuf, fsum, uh,
            rsend, rrecv, csend, crecv, ksend, krecv, frr, fcs, fcr, fks, fkr, fce, fke,
            asend, arecv, bsend, brecv,
@@ -241,9 +241,11 @@
             for h in range(2):
                 ksend[v, h] = pack(sides[h][part], 96 * h)
 
-    def start_edges(r, par):
+    def start_columns(r, par):
         for h in range(2):
             col_copy(h, r, par, into[h]).start()
+
+    def start_rows(r, par):
         if r == 0 or r == nb - 1:
             v = 0 if r == 0 else 1
             row_copy(v, par, 1 - v).start()
@@ -267,6 +269,8 @@
             share_copy(o, par, j).start()
 
     def row_fog(par):
+        for o in range(1, ngx):
+            fog_copy(o, par, i).wait_send()
         for o in range(1, ngy):
             share_copy(o, par, lax.rem(j + o, ngy)).wait_recv()
         total = jnp.zeros((nj, 128), F32)
@@ -354,7 +358,7 @@
         put_blur(rows, left, x[:, :128])
         put_blur(rows, right, x[:, 128:])
 
-    def blur_ends(par, use):
+    def blur_ends(par, use, between):
         half = nb // 2
         for h in range(2):
             cor_copy(0, h, par, 0, h).wait_recv()
@@ -366,6 +370,7 @@
         for r in range(half + 1):
             put_ends(PAD + r * RB, get_columns(r, par))
         use([(r, first_dot(r, pick_ends)) for r in range(half)])
+        between()
         for h in range(2):
             cor_copy(1, h, par, 1, h).wait_recv()
             for r in range(half + 1, nb):
@@ -408,12 +413,11 @@
                     sides.append(x)
                 fill_edges(r, sides, f[rows, center] * d[rows, center])
             for r, _ in backs:
-                start_edges(r, nxt)
-
-        blur_ends(par, use)
-        for o in range(1, ngx):
-            fog_copy(o, par, i).wait_send()
-        row_fog(par)
+                start_columns(r, nxt)
+            for r, _ in backs:
+                start_rows(r, nxt)
+
+        blur_ends(par, use, lambda: row_fog(par))
         for o in range(1, ngy):
             share_copy(o, par, j).wait_send()
         send_share(reduce_acc(), nxt)
@@ -486,6 +490,18 @@
         jnp.sum(jnp.sum(total, axis=0, keepdims=True), axis=1, keepdims=True), (1, 128))
     share = reduce_acc()
 
+    pl.semaphore_wait(barrier, len(partners))
+    for r in range(nb):
+        start_columns(r, 0)
+        start_rows(r, 0)
+    send_share(share, 0)
+    for o in range(1, ngx):
+        fog_copy(o, 1, i).start()
+    for v in range(2):
+        frow_copy(v, 1 - v).start()
+        fcol_copy(v, into[v]).start()
+        for h in range(2):
+            fcor_copy(v, h, 1 - v, into[h]).start()
     for c in consts:
         c.wait()
     for r in range(nb):
@@ -499,17 +515,6 @@
             u = first_dot(r, lambda ref, win: ref[win, cs])
             w[rows, cs] = u + 0.75 * f[rows, cs] - 1.0
 
-    pl.semaphore_wait(barrier, len(partners))
-    for r in range(nb):
-        start_edges(r, 0)
-    send_share(share, 0)
-    for o in range(1, ngx):
-        fog_copy(o, 1, i).start()
-    for v in range(2):
-        frow_copy(v, 1 - v).start()
-        fcol_copy(v, into[v]).start()
-        for h in range(2):
-            fcor_copy(v, h, 1 - v, into[h]).start()
     for r in range(nb):
         rows = slice(r * RB, r * RB + RB)
         put_charge(r, slice(0, breadth), f[rows, :] * d[rows, :])
@@ -541,17 +546,10 @@
                 d[rows, cs] = now - own
                 out_r[rows, cs] = fog_rows(r, change, cs)
 
-    blur_ends(par, use_last)
-    for o in range(1, ngx):
-        fog_copy(o, par, i).wait_send()
     row_fog(par)
+    blur_ends(par, use_last, lambda: None)
     get_fog(par)
-    last = wide(fog_at(1, blk_j), breadth // 128)
-    for r in range(nb):
-        rows = slice(r * RB, r * RB + RB)
-        change = out_r[rows, :] - last
-        d[rows, :] = d[rows, :] + change
-        out_r[rows, :] = change * (1.0 / 1.5)
+    out_g[...] = fog_at(1, blk_j)
     for v in range(2):
         frow_copy(v, v).wait_send()
         fcol_copy(v, v).wait_send()
@@ -577,11 +575,11 @@
     any_spec = pl.BlockSpec(memory_space=pltpu.HBM)
     tile, padded = (height, breadth), (height + 2 * PAD, breadth)
     rows, cols, corners = (2, PAD, breadth), (2, nb, RB // 4, 128), (2, 2, PAD // 4, 128)
-    return pl.pallas_call(
+    dose_map, change, last = pl.pallas_call(
         functools.partial(kernel, ngx, ngy),
-        out_shape=(vm(tile, F32), vm(tile, F32)),
+        out_shape=(vm(tile, F32), vm(tile, F32), vm((1, 128), F32)),
         in_specs=[any_spec] * 8,
-        out_specs=(pl.BlockSpec(memory_space=vm), pl.BlockSpec(memory_space=vm)),
+        out_specs=(pl.BlockSpec(memory_space=vm),) * 3,
         scratch_shapes=[
             vm(tile, jnp.int32), vm(tile, F32), vm(tile, F32),
             vm(a1.shape, BF), vm(w2.shape, BF), vm(wh.shape, BF), vm(ah.shape, BF), vm(qc.shape, F32), vm(pc.shape, F32),
@@ -602,6 +600,8 @@
         ),
     )(coverage, dose, jnp.asarray(a1), jnp.asarray(w2), jnp.asarray(wh), jnp.asarray(ah),
       jnp.asarray(qc, F32), jnp.asarray(pc, F32))
+    change = change - last[0, 0]
+    return dose_map + change, change * (1.0 / 1.5)
 
 
 def solution(mesh):

time: 62.5 us -> 59.9 us (0.958)
  other arithmetic: 0 us -> 2.75 us
  Pallas kernels: 59.1 us -> 56.4 us
  local copies, waits for them, and re-layouts: 2.64 us -> 0 us
    mul x0 -> x1, other arithmetic: none -> 2.75 us  [per_device(): return (dose_map + change, change * (1.0 / 1.5))]
    pallas_call x1, Pallas kernels: 59.1 us -> 56.4 us  [per_device(): pl.pallas_call(functools.partial(kernel, ngx, ngy), out_shape=(vm(tile, F...]
    unnamed x2 -> x0, local copies, waits for them, and re-layouts: 2.64 us -> none
where the time goes in v4:
time: 59.9 us; the launch traced here: 59.8 us
  Pallas kernels  56.4 us (94%)
  other arithmetic  2.75 us (5%)
  between operations  0.64 us (1%)
    pallas_call x1, Pallas kernels, per_device(): pl.pallas_call(functools.partial(kernel, ngx, ngy), out_shape=(vm(tile, F...  56.4 us
    mul x1, other arithmetic, per_device(): return (dose_map + change, change * (1.0 / 1.5))  2.75 us

profile of v4, /device:TPU:1, one launch (start us, length us, event | category | flops | bytes accessed | tf_op | source)
XLA Modules:
  0.0 59.8 jit_solution(10591004927055994393)
XLA Ops:
  0.6 56.4 %shard_map.95 = (f32[1024,512]{1,0:T(8,128)S(1)}, f32[1024,512]{1,0:T(8,128)S(1)}, f32[1,128]{1,0:T(1,128)S(1)}) custom-call(s32[1024,512]{1,0:T(8,128)} %cover_hbm.1, f32[1024,512]{1,0:T(8,128)} %dose_hbm.1, bf16[256,960]{1,0:T(8,128)(2,1)} %constant.14.clone.a1_hbm, bf16[2,1152,256]{2,1,0:T(8,128)(2,1)} %constant.15.clone.w2_hbm, ...), custom_call_target="tpu_custom_call" | custom-call | tf_op jit(solution)/shard_map/pallas_call | solution.py:578
  57.0 2.8 %subtract_multiply_fusion = (f32[1024,512]{1,0:T(8,128)}, f32[1024,512]{1,0:T(8,128)}) fusion(f32[1024,512]{1,0:T(8,128)S(1)} %get-tuple-element.6, f32[]{:T(128)S(1)} %bitcast.2, f32[1024,512]{1,0:T(8,128)S(1)} %get-tuple-element.5), kind=kLoop, calls=%fused_computation | loop fusion | flops 1572864 | bytes 8388612 | tf_op jit(solution)/shard_map/mul | solution.py:604
